TPU v7x, 512 devices: a whole 4x8x8 slice. The times are simulated.
512 devices in a mesh: tensor: 8 (over y), expert: 64 (over x, z, core).
Axes of the slice: x: 4, y: 8, z: 8, core: 2. Of those that a mesh axis runs over, the one named last changes fastest.
Arguments:
- tokens: bfloat16 [4096, 4096], P('expert', 'tensor'), may hold values from -6 to 6
- gate_weight: bfloat16 [64, 1536, 4096], P('expert', 'tensor'), may hold values from -0.09375 to 0.09375
- up_weight: bfloat16 [64, 1536, 4096], P('expert', 'tensor'), may hold values from -0.09375 to 0.09375
- down_weight: bfloat16 [64, 1536, 4096], P('expert', None, 'tensor'), may hold values from -0.15625 to 0.15625
- expert_ids: int32 [4096, 8], P('expert'), may hold values from 0 to 63, all different within a row; in each aligned block of 64 rows (0 to 63, 64 to 127, ...) at most 16 rows name the same one
- gate_probs: float32 [4096, 8], P('expert'), may hold values from 0.05 to 0.25
Outputs:
- mixed: bfloat16 [4096, 4096], P('expert', 'tensor')
Inputs may be any that keep to these rules, and one draw needn't show every extreme that they name: `expert_ids`: in each aligned block of 64 rows (the tokens of one index of expert) no expert is named by more than 16 rows, a bound that some block reaches; the 8 experts of a row differ.
All inputs are finite; a program needn't handle non-finite values.
Results may differ from a plain program's by a relative error of at most 0.0057.
Values may be sent and summed in bfloat16 or wider, within the bound.
A program may use at most 64 MiB of HBM per device.

v0:
```python
import jax
import jax.numpy as jnp
from jax import lax
from jax.sharding import PartitionSpec as P


def local(tokens, gate_weight, up_weight, down_weight, expert_ids, gate_probs):
    rows = tokens.shape[0]
    experts = lax.axis_size("expert")
    top = expert_ids.shape[1]
    slot_count = min(rows * top * 2 // experts, rows * 3 // 4)
    flat = expert_ids.reshape(rows * top)
    onehot = (flat[:, None] == jnp.arange(experts, dtype=jnp.int32)[None, :]).astype(jnp.int32)
    before = jnp.cumsum(onehot, axis=0) - onehot
    slots = jnp.sum(before * onehot, axis=1)
    target = (flat * slot_count + slots).reshape(rows, top)
    columns = jnp.arange(experts * slot_count, dtype=jnp.int32)
    match = target[None, :, :] == columns[:, None, None]
    pick = jnp.any(match, axis=2).astype(jnp.bfloat16)
    weight = jnp.sum(match.astype(jnp.float32) * gate_probs[None, :, :], axis=2)
    contract = (((1,), (1,)), ((), ()))
    whole = lax.all_gather(tokens, "tensor", axis=1, tiled=True)
    sent = jnp.dot(pick, whole, preferred_element_type=jnp.float32).astype(jnp.bfloat16)
    sent = sent.reshape(experts, slot_count, whole.shape[1])
    arrived = lax.all_to_all(sent, "expert", split_axis=0, concat_axis=0, tiled=True).reshape(
        experts * slot_count, whole.shape[1]
    )
    gate = lax.dot_general(arrived, gate_weight[0], contract, preferred_element_type=jnp.float32)
    up = lax.dot_general(arrived, up_weight[0], contract, preferred_element_type=jnp.float32)
    hidden = (jax.nn.silu(gate) * up).astype(jnp.bfloat16)
    out_cols = down_weight.shape[2]
    part_down = down_weight[0]
    output = jnp.dot(
        lax.all_gather(hidden, "tensor", axis=1, tiled=True),
        part_down,
        preferred_element_type=jnp.float32,
    ).astype(jnp.bfloat16)
    returned = lax.all_to_all(
        output.reshape(experts, slot_count, out_cols),
        "expert",
        split_axis=0,
        concat_axis=0,
        tiled=True,
    )
    returned = returned.reshape(experts * slot_count, out_cols).astype(jnp.float32)
    mixed = lax.dot_general(
        weight, returned, (((0,), (0,)), ((), ())), precision=lax.Precision.HIGHEST
    )
    return mixed.astype(jnp.bfloat16)


def solution(mesh):
    in_specs = (
        P("expert", "tensor"),
        P("expert", "tensor", None),
        P("expert", "tensor", None),
        P("expert", None, "tensor"),
        P("expert", None),
        P("expert", None),
    )
    out_specs = P("expert", "tensor")
    return jax.shard_map(local, mesh=mesh, in_specs=in_specs, out_specs=out_specs, check_vma=False)
```

profile of v0, /device:TPU:1, one launch (start us, length us, event | category | flops | bytes accessed | tf_op | source)
XLA Modules:
  0.0 343.1 jit_solution(10450527838432070093)
XLA Ops:
  6.5 0.0 copy-start
  6.5 0.0 all-gather.2.cloned.1.call-start
  6.5 0.9 copy.21
  7.4 0.1 eq.42
  7.5 0.1 eq.38
  7.6 1.2 reduce-window.6
  8.8 0.2 slice_reduce_fusion
  9.1 0.1 fusion.18
  9.2 0.1 reduce_sum.21
  9.3 0.1 copy.24
  9.4 0.7 multiply_add_fusion
  10.1 0.1 copy.25
  10.2 0.7 fusion
  10.9 21.9 %all_gather.6 = bf16[64,4096]{1,0:T(8,128)(2,1)S(1)} all-gather(bf16[64,512]{1,0:T(8,128)(2,1)} %param.6), channel_id=1, replica_groups=mesh['tensor'=8,'expert'=64] {'tensor'}, dimensions={1}, use_global_device_ids=true | all-gather | bytes 589824 | tf_op jit(solution)/shard_map/all_gather | solution.py:22
  32.8 2.4 convolution_convert_fusion
  35.2 0.0 copy-start.2
  35.2 206.0 %all_to_all.10 = bf16[64,16,4096]{2,1,0:T(8,128)(2,1)S(1)} all-to-all(bf16[64,16,4096]{2,1,0:T(8,128)(2,1)S(1)} %bitcast.45), channel_id=1, replica_groups=mesh['tensor'=8,'expert'=64] {'expert'}, dimensions={0} | all-to-all | bytes 16777216 | tf_op jit(solution)/shard_map/all_to_all | solution.py:25
  241.3 0.0 copy-done.2
  241.3 0.0 copy-start.3
  241.3 2.9 fusion.5
  244.2 0.0 copy-done.3
  244.2 3.7 %fusion.13 = bf16[1024,192]{0,1:T(8,128)(2,1)} fusion(bf16[1024,4096]{1,0:T(8,128)(2,1)S(1)} %bitcast.47, bf16[1,192,4096]{2,1,0:T(8,128)(2,1)S(1)} %copy-done.3, f32[1024,192]{0,1:T(8,128)S(1)} %fusion.5), kind=kOutput, calls=%fused_computation.12 | convolution fusion | flops 1611792384 | bytes 11141120 | tf_op jit(solution)/shard_map/dot_general | solution.py:29
  247.9 0.0 all-gather.2.cloned.1.call-update
  247.9 42.1 %all-gather.2.cloned.1.call-done = bf16[1024,1536]{0,1:T(8,128)(2,1)} async-done(((bf16[1024,192]{0,1:T(8,128)(2,1)}), bf16[1024,1536]{0,1:T(8,128)(2,1)}) %all-gather.2.cloned.1.call-update) | async-done | bytes 3145744 | tf_op jit(solution)/shard_map/all_gather | solution.py:34
  290.0 0.0 copy-done
  290.0 4.7 %fusion.7 = bf16[1024,512]{1,0:T(8,128)(2,1)} fusion(bf16[1024,1536]{0,1:T(8,128)(2,1)} %all-gather.2.cloned.1.call-done, bf16[1,1536,512]{2,1,0:T(8,128)(2,1)S(1)} %copy-done), kind=kOutput, calls=%fused_computation.10 | convolution fusion | flops 1611137024 | bytes 5767168 | tf_op jit(solution)/shard_map/dot_general | solution.py:33
  294.7 0.0 copy-start.1
  294.7 11.7 %all-to-all-start.1 = ((bf16[64,16,512]{2,1,0:T(8,128)(2,1)}), bf16[64,16,512]{2,1,0:T(8,128)(2,1)S(1)}, u32[]{:S(2)}, u32[]{:S(2)}) async-start(bf16[64,16,512]{2,1,0:T(8,128)(2,1)} %bitcast.49), calls=%async_computation.1 | async-start | bytes 2097152 | tf_op jit(solution)/shard_map/all_to_all | solution.py:38
  306.4 0.0 copy-done.1
  306.5 0.1 copy.26
  306.5 0.7 select_reduce_fusion
  307.3 27.7 %all-to-all-done.1 = bf16[64,16,512]{2,1,0:T(8,128)(2,1)S(1)} async-done(((bf16[64,16,512]{2,1,0:T(8,128)(2,1)}), bf16[64,16,512]{2,1,0:T(8,128)(2,1)S(1)}, u32[]{:S(2)}, u32[]{:S(2)}) %all-to-all-start.1) | async-done | bytes 1048608 | tf_op jit(solution)/shard_map/all_to_all | solution.py:38
  335.0 1.3 convolution_convert_fusion.1
  (3 shorter events, 0.1 us)
Async XLA Ops:
  6.5 283.4 %copy-start = (bf16[1,1536,512]{2,1,0:T(8,128)(2,1)S(1)}, bf16[1,1536,512]{2,1,0:T(8,128)(2,1)}, u32[]{:S(2)}) copy-start(bf16[1,1536,512]{2,1,0:T(8,128)(2,1)} %param.9) | copy-start | bytes 4718596
  6.5 283.4 %all-gather.2.cloned.1.call-start = ((), (), s32[]{:S(2)}) async-start(), calls=%async_computation.2 | async-start | bytes 3538944 | tf_op jit(solution)/shard_map/all_gather | solution.py:34
  35.2 206.1 %copy-start.2 = (bf16[1,192,4096]{2,1,0:T(8,128)(2,1)S(1)}, bf16[1,192,4096]{2,1,0:T(8,128)(2,1)}, u32[]{:S(2)}) copy-start(bf16[1,192,4096]{2,1,0:T(8,128)(2,1)} %param.7) | copy-start | bytes 4718596
  241.3 2.9 copy-start.3
  294.7 11.8 %copy-start.1 = (f32[64,8]{0,1:T(8,128)S(1)}, f32[64,8]{0,1:T(8,128)}, u32[]{:S(2)}) copy-start(f32[64,8]{0,1:T(8,128)} %param.11) | copy-start | bytes 6148
  294.7 40.3 %all-to-all-start.1 = ((bf16[64,16,512]{2,1,0:T(8,128)(2,1)}), bf16[64,16,512]{2,1,0:T(8,128)(2,1)S(1)}, u32[]{:S(2)}, u32[]{:S(2)}) async-start(bf16[64,16,512]{2,1,0:T(8,128)(2,1)} %bitcast.49), calls=%async_computation.1 | async-start | bytes 2097152 | tf_op jit(solution)/shard_map/all_to_all | solution.py:38
Sparse Core Ops, SparseCore 0:
  248.0 41.8 all-gather.1
where the time goes:
time: 343 us
  blocking collectives  228 us (66%)
  waiting for transfers between devices  69.8 us (20%)
  matrix products  15 us (4%)
  between operations  13.5 us (4%)
  starting transfers between devices  11.7 us (3%)
  other arithmetic  3.49 us (1%)
    all_to_all x1, blocking collectives, local(): lax.all_to_all(sent, 'expert', split_axis=0, concat_axis=0, tiled=True)  206 us
    all_gather x1, waiting for transfers between devices, local(): lax.all_gather(hidden, 'tensor', axis=1, tiled=True)  42.1 us
    all_to_all x1, waiting for transfers between devices, local(): lax.all_to_all(output.reshape(experts, slot_count, out_cols), 'expert', s...  27.7 us
    all_gather x1, blocking collectives, local(): whole = lax.all_gather(tokens, 'tensor', axis=1, tiled=True)  21.9 us
    all_to_all x1, starting transfers between devices, local(): lax.all_to_all(output.reshape(experts, slot_count, out_cols), 'expert', s...  11.7 us
  transfers between devices with their start and end apart: 2, of which 2 were waited for; matrix products, arithmetic and copies ran while one was open for 0% of the time, Pallas kernels for 0%

commit v1 on v0

v1 whole, which is shorter than its diff:
```python
import functools

import jax
import jax.numpy as jnp
from jax import lax
from jax.experimental import pallas as pl
from jax.experimental.pallas import tpu as pltpu
from jax.sharding import PartitionSpec as P

MESH = pl.DeviceIdType.MESH
BF16 = jnp.bfloat16
F32 = jnp.float32
NX, NY, NZ, NC = 4, 8, 8, 2
ROW = NX * NC
ROWS = 64
SLOTS = 16
SLICE = 512
HALF = 2048
HID = 192
PIECE = HID // 2
META = 128
GROUPS = 4


def dot(a, b, da, db):
    return lax.dot_general(a, b, (((da,), (db,)), ((), ())), preferred_element_type=F32)


def kernel(
    tok, gate, up, down, ids, prob, out,
    blocks, picked, arrived, weights, down_v, own, part_out, part_in,
    hidden, outputs, returned, sums_out, sums_in, own_sum,
    pg_s, pg_r, w_s, w_r, lw, ld, z_s, z_r, x_s, x_r, p_s, p_r, h_s, h_r, o_s, o_r, f_s, f_r,
):
    t = lax.axis_index("tensor")
    e = lax.axis_index("expert")
    c = lax.rem(e, NC)
    z = lax.rem(e // NC, NZ)
    x = e // (NC * NZ)
    me = x * NC + c
    q = lax.rem(t, 2)

    def along_y(step):
        return (lax.rem(t + step + NY, NY), e)

    def along_z(step):
        return (t, (x * NZ + lax.rem(z + step + NZ, NZ)) * NC + c)

    def in_row(j):
        return (t, ((j // NC) * NZ + z) * NC + lax.rem(j, NC))

    def other(i):
        return lax.rem(me + i, ROW)

    def send(src, dst, ss, rs, dev):
        return pltpu.make_async_remote_copy(
            src_ref=src, dst_ref=dst, send_sem=ss, recv_sem=rs, device_id=dev, device_id_type=MESH
        )

    def got(ref, sem):
        send(ref, ref, sem, sem, along_y(1)).wait_recv()

    def sent(ref, sem):
        send(ref, ref, sem, sem, along_y(1)).wait_send()

    def offset(d):
        return ((d + 1) // 2) * (1 - 2 * lax.rem(d + 1, 2))

    barrier = pltpu.get_barrier_semaphore()
    for step in (1, 7, 2, 6, 4):
        pl.semaphore_signal(barrier, inc=1, device_id=along_y(step), device_id_type=MESH)
    for i in range(1, ROW):
        pl.semaphore_signal(barrier, inc=1, device_id=in_row(other(i)), device_id_type=MESH)
    for step in range(1, NZ):
        pl.semaphore_signal(barrier, inc=1, device_id=along_z(step), device_id_type=MESH)
    def column(j, parity):
        return pl.ds(pl.multiple_of((2 * j + parity) * SLICE, SLICE), SLICE)

    local = []
    for a, ref in enumerate((gate, up)):
        for j in range(4):
            local.append(
                pltpu.make_async_copy(
                    ref.at[:, column(j, q)],
                    weights.at[pl.ds(a * HID, HID), pl.ds(j * SLICE, SLICE)],
                    lw.at[a, j],
                )
            )
    local.append(pltpu.make_async_copy(down, down_v, ld.at[0]))
    for cp in local:
        cp.start()
    pl.semaphore_wait(barrier, 5 + 7 + 7)

    my_cols = pl.ds(pl.multiple_of((t // 2) * SLICE, SLICE), SLICE)
    for i in range(1, 4):
        send(tok, blocks.at[0, :, my_cols], pg_s.at[i - 1], pg_r.at[i - 1], along_y(2 * i)).start()
    blocks[0, :, my_cols] = tok[...]

    lane = lax.broadcasted_iota(jnp.int32, (ROWS, META), 1).astype(F32)
    idf = ids[...].astype(F32)
    pf = prob[...]
    named = jnp.zeros((ROWS, META), F32)
    for k in range(8):
        named = named + (lane == idf[:, k : k + 1]).astype(F32)
    earlier = (
        lax.broadcasted_iota(jnp.int32, (ROWS, ROWS), 1)
        < lax.broadcasted_iota(jnp.int32, (ROWS, ROWS), 0)
    ).astype(F32)
    before = dot(earlier.astype(BF16), named.astype(BF16), 1, 0)
    meta = jnp.zeros((ROWS, META), F32)
    p_hi = pf.astype(BF16).astype(F32)
    p_lo = pf - p_hi
    for k in range(8):
        ek = idf[:, k : k + 1]
        slot = jnp.sum(jnp.where(lane == ek, before, 0.0), axis=1, keepdims=True)
        meta = jnp.where(lane == float(k), ek, meta)
        meta = jnp.where(lane == float(8 + k), slot, meta)
        meta = jnp.where(lane == float(16 + k), p_hi[:, k : k + 1], meta)
        meta = jnp.where(lane == float(24 + k), p_lo[:, k : k + 1], meta)
    blocks[0, :, pl.ds(HALF, META)] = meta.astype(BF16)
    for i in range(1, 4):
        src = lax.rem(t - 2 * i + NY, NY)
        cols = pl.ds(pl.multiple_of((src // 2) * SLICE, SLICE), SLICE)
        got(blocks.at[0, :, cols], pg_r.at[i - 1])

    lane_i = lax.broadcasted_iota(jnp.int32, (ROWS, META), 1)
    lane_j = lane_i // SLOTS
    lane_e = ((lane_j // NC) * NZ + z) * NC + lax.rem(lane_j, NC)
    lane_code = (lane_e * SLOTS + lax.rem(lane_i, SLOTS)).astype(F32)

    def matches(m):
        return [
            (m[:, k : k + 1] * float(SLOTS) + m[:, 8 + k : 9 + k]) == lane_code for k in range(8)
        ]

    def pass_on(d, whole_to, direction):
        send(
            blocks.at[d], blocks.at[whole_to], z_s.at[whole_to], z_r.at[whole_to], along_z(direction)
        ).start()

    def block_step(d, _):
        @pl.when(jnp.logical_and(d >= 1, d <= 6))
        def _():
            got(blocks.at[d], z_r.at[d])

        @pl.when(d == 7)
        def _():
            got(blocks.at[7, pl.ds(0, 32)], z_r.at[7])
            got(blocks.at[7, pl.ds(32, 32)], z_r.at[8])

        @pl.when(d == 0)
        def _():
            pass_on(0, 1, -1)
            pass_on(0, 2, 1)

        @pl.when(jnp.logical_and(d >= 1, d <= 4))
        def _():
            pass_on(d, d + 2, 1 - 2 * lax.rem(d, 2))

        @pl.when(d == 5)
        def _():
            half = pl.ds(0, 32)
            send(blocks.at[5, half], blocks.at[7, half], z_s.at[7], z_r.at[7], along_z(-1)).start()

        @pl.when(d == 6)
        def _():
            half = pl.ds(32, 32)
            send(blocks.at[6, half], blocks.at[7, half], z_s.at[8], z_r.at[8], along_z(1)).start()

        m = blocks[d, :, pl.ds(HALF, META)].astype(F32)
        pick = functools.reduce(jnp.logical_or, matches(m))
        pick = jnp.where(pick, 1.0, 0.0).astype(BF16)
        rows = dot(pick, blocks[d, :, pl.ds(0, HALF)], 0, 0).astype(BF16)
        picked[d] = rows.reshape(ROW, SLOTS, HALF)
        g = d // 2
        at = pl.ds(pl.multiple_of(lax.rem(d, 2) * SLOTS, SLOTS), SLOTS)
        arrived[g, me, at] = picked[d, me]
        for i in range(1, ROW):
            j = other(i)
            send(
                picked.at[d, j], arrived.at[g, me, at], x_s.at[d, j], x_r.at[d, me], in_row(j)
            ).start()
        return 0

    block_step(0, 0)

    for a, ref in enumerate((gate, up)):
        for j in range(4):
            cols = column(j, 1 - q)
            to = pl.ds(j * SLICE, SLICE)
            send(
                ref.at[pl.ds(0, PIECE), cols],
                weights.at[pl.ds(3 * HID + a * PIECE, PIECE), to],
                w_s.at[0, a, j], w_r.at[0, a, j], along_y(-1),
            ).start()
            send(
                ref.at[pl.ds(PIECE, PIECE), cols],
                weights.at[pl.ds(2 * HID + a * PIECE, PIECE), to],
                w_s.at[1, a, j], w_r.at[1, a, j], along_y(1),
            ).start()

    lax.fori_loop(1, 5, block_step, 0)

    for cp in local:
        cp.wait()
    for a in range(2):
        for j in range(4):
            to = pl.ds(j * SLICE, SLICE)
            got(weights.at[pl.ds(3 * HID + a * PIECE, PIECE), to], w_r.at[0, a, j])
            got(weights.at[pl.ds(2 * HID + a * PIECE, PIECE), to], w_r.at[1, a, j])

    def partials(g):
        for dl in range(2):
            for i in range(1, ROW):
                src = other(i)
                got(arrived.at[g, src, pl.ds(dl * SLOTS, SLOTS)], x_r.at[2 * g + dl, src])
        rows = arrived[g].reshape(2 * ROW * SLOTS, HALF)
        for side in range(2):
            w = weights[pl.ds((2 + side) * HID, HID)]
            part_out[g, side] = dot(w, rows, 1, 1).astype(BF16)
            send(
                part_out.at[g, side], part_in.at[g, 1 - side],
                p_s.at[g, side], p_r.at[g, 1 - side], along_y(2 * side - 1),
            ).start()
        for a in range(2):
            own[pl.ds(a * HID, HID)] = dot(weights[pl.ds(a * HID, HID)], rows, 1, 1)

    def activate(g):
        for side in range(2):
            got(part_in.at[g, side], p_r.at[g, side])
            lo = pl.ds(side * PIECE, PIECE)
            gv = own[lo] + part_in[g, side, pl.ds(0, PIECE)].astype(F32)
            uv = own[pl.ds(HID + side * PIECE, PIECE)] + part_in[
                g, side, pl.ds(PIECE, PIECE)
            ].astype(F32)
            hidden[g, t, lo] = (gv / (1.0 + jnp.exp(-gv)) * uv).astype(BF16)
        for way in range(2):
            send(
                hidden.at[g, t], hidden.at[g, t], h_s.at[g, way, 0], h_r.at[g, way, 0],
                along_y(1 - 2 * way),
            ).start()

    def forward(g, h):
        for way in range(2):
            src = lax.rem(t + (h if way else NY - h), NY)
            ref = hidden.at[g, src]
            got(ref, h_r.at[g, way, h - 1])
            if h == 3:
                ref = hidden.at[g, src, pl.ds(way * PIECE, PIECE)]
            send(ref, ref, h_s.at[g, way, h], h_r.at[g, way, h], along_y(1 - 2 * way)).start()

    def project(g):
        far = lax.rem(t + 4, NY)
        for way in range(2):
            got(hidden.at[g, far, pl.ds(way * PIECE, PIECE)], h_r.at[g, way, 3])
        h = hidden[g].reshape(NY * HID, 2 * ROW * SLOTS)
        o = dot(h, down_v[...], 0, 0).astype(BF16)
        outputs[g] = o.reshape(ROW, 2 * SLOTS, SLICE)
        returned[g, me] = outputs[g, me]
        for i in range(1, ROW):
            j = other(i)
            send(
                outputs.at[g, j], returned.at[g, me], o_s.at[g, j], o_r.at[g, me], in_row(j)
            ).start()

    def combine(g):
        for i in range(1, ROW):
            src = other(i)
            got(returned.at[g, src], o_r.at[g, src])
        for dl in range(2):
            d = 2 * g + dl
            m = blocks[d, :, pl.ds(HALF, META)].astype(F32)
            hi = jnp.zeros((ROWS, META), F32)
            lo = jnp.zeros((ROWS, META), F32)
            for k, match in enumerate(matches(m)):
                hi = jnp.where(match, m[:, 16 + k : 17 + k], hi)
                lo = jnp.where(match, m[:, 24 + k : 25 + k], lo)
            vals = returned[g, :, pl.ds(dl * SLOTS, SLOTS)].reshape(ROW * SLOTS, SLICE)
            total = dot(hi.astype(BF16), vals, 1, 0) + dot(lo.astype(BF16), vals, 1, 0)
            sums_out[d] = total.astype(BF16)

            @pl.when(d == 0)
            def _():
                own_sum[...] = total

            @pl.when(d > 0)
            def _():
                send(
                    sums_out.at[d], sums_in.at[d], f_s.at[d], f_r.at[d], along_z(offset(d))
                ).start()

    def group_step(g, _):
        late = jnp.logical_and(g >= 1, g <= GROUPS)

        @pl.when(g < GROUPS)
        def _():
            partials(g)

        @pl.when(g == 0)
        def _():
            lax.fori_loop(5, 7, block_step, 0)

        @pl.when(g == 1)
        def _():
            block_step(7, 0)

        @pl.when(late)
        def _():
            forward(g - 1, 2)

        @pl.when(g < GROUPS)
        def _():
            activate(g)

        @pl.when(g >= 2)
        def _():
            combine(g - 2)

        @pl.when(late)
        def _():
            forward(g - 1, 3)

        @pl.when(g < GROUPS)
        def _():
            forward(g, 1)

        @pl.when(late)
        def _():
            project(g - 1)

        return 0

    lax.fori_loop(0, GROUPS + 2, group_step, 0)

    total = own_sum[...]
    for d in range(1, NZ):
        got(sums_in.at[d], f_r.at[d])
        total = total + sums_in[d].astype(F32)
    out[...] = total.astype(BF16)

    for i in range(3):
        sent(tok, pg_s.at[i])
    for a in range(2):
        for j in range(4):
            for way in range(2):
                sent(weights.at[pl.ds(0, PIECE), pl.ds(0, SLICE)], w_s.at[way, a, j])
    for d in range(1, 7):
        sent(blocks.at[d], z_s.at[d])
    for d in (7, 8):
        sent(blocks.at[7, pl.ds(0, 32)], z_s.at[d])

    def drain_x(d, _):
        for i in range(1, ROW):
            j = other(i)
            sent(picked.at[d, j], x_s.at[d, j])
        return 0

    lax.fori_loop(0, NZ, drain_x, 0)

    def drain_group(g, _):
        for side in range(2):
            sent(part_out.at[g, side], p_s.at[g, side])
            for h in range(3):
                sent(hidden.at[g, 0], h_s.at[g, side, h])
            sent(hidden.at[g, 0, pl.ds(0, PIECE)], h_s.at[g, side, 3])
        for i in range(1, ROW):
            j = other(i)
            sent(outputs.at[g, j], o_s.at[g, j])
        return 0

    lax.fori_loop(0, GROUPS, drain_group, 0)
    for d in range(1, NZ):
        sent(sums_out.at[d], f_s.at[d])


def local(tokens, gate_weight, up_weight, down_weight, expert_ids, gate_probs):
    hbm = pl.BlockSpec(memory_space=pl.ANY)
    vmem = pl.BlockSpec(memory_space=pltpu.VMEM)
    dma = pltpu.SemaphoreType.DMA
    group_rows = 2 * ROW * SLOTS
    scratch = [
        pltpu.VMEM((NZ, ROWS, HALF + META), BF16),
        pltpu.VMEM((NZ, ROW, SLOTS, HALF), BF16),
        pltpu.VMEM((GROUPS, ROW, 2 * SLOTS, HALF), BF16),
        pltpu.VMEM((4 * HID, HALF), BF16),
        pltpu.VMEM((NY * HID, SLICE), BF16),
        pltpu.VMEM((2 * HID, group_rows), F32),
        pltpu.VMEM((GROUPS, 2, HID, group_rows), BF16),
        pltpu.VMEM((GROUPS, 2, HID, group_rows), BF16),
        pltpu.VMEM((GROUPS, NY, HID, group_rows), BF16),
        pltpu.VMEM((GROUPS, ROW, 2 * SLOTS, SLICE), BF16),
        pltpu.VMEM((GROUPS, ROW, 2 * SLOTS, SLICE), BF16),
        pltpu.VMEM((NZ, ROWS, SLICE), BF16),
        pltpu.VMEM((NZ, ROWS, SLICE), BF16),
        pltpu.VMEM((ROWS, SLICE), F32),
        dma((3,)), dma((3,)),
        dma((2, 2, 4)), dma((2, 2, 4)), dma((2, 4)), dma((1,)),
        dma((9,)), dma((9,)),
        dma((NZ, ROW)), dma((NZ, ROW)),
        dma((GROUPS, 2)), dma((GROUPS, 2)),
        dma((GROUPS, 2, 4)), dma((GROUPS, 2, 4)),
        dma((GROUPS, ROW)), dma((GROUPS, ROW)),
        dma((NZ,)), dma((NZ,)),
    ]
    return pl.pallas_call(
        kernel,
        out_shape=jax.ShapeDtypeStruct((ROWS, SLICE), BF16),
        in_specs=[vmem, hbm, hbm, hbm, vmem, vmem],
        out_specs=vmem,
        scratch_shapes=scratch,
        compiler_params=pltpu.CompilerParams(
            collective_id=0, has_side_effects=True, vmem_limit_bytes=48 << 20
        ),
        cost_estimate=pl.CostEstimate(flops=5_000_000_000, bytes_accessed=5_000_000, transcendentals=200_000),
    )(tokens, gate_weight[0], up_weight[0], down_weight[0], expert_ids, gate_probs)


def solution(mesh):
    in_specs = (
        P("expert", "tensor"),
        P("expert", "tensor", None),
        P("expert", "tensor", None),
        P("expert", None, "tensor"),
        P("expert", None),
        P("expert", None),
    )
    out_specs = P("expert", "tensor")
    return jax.shard_map(local, mesh=mesh, in_specs=in_specs, out_specs=out_specs, check_vma=False)
```

time: 343 us -> 130 us (0.38)
  the two profiles are of different devices: /device:TPU:1 before, /device:TPU:64 now
where the time goes in v1:
time: 130 us; the launch traced here: 129 us
  Pallas kernels  122 us (94%)
  local copies, waits for them, and re-layouts  7.23 us (6%)
    pallas_call x1, Pallas kernels, local(): pl.pallas_call(kernel, out_shape=jax.ShapeDtypeStruct((ROWS, SLICE), BF16...  122 us
    unnamed x11, local copies, waits for them, and re-layouts  7.23 us

profile of v1, /device:TPU:64, one launch (start us, length us, event | category | flops | bytes accessed | tf_op | source)
XLA Modules:
  0.0 129.5 jit_solution(14494883903209274311)
XLA Ops:
  0.0 0.8 copy.7.ids
  0.8 0.8 copy.8.prob
  1.5 0.0 copy-start
  1.5 1.4 %copy-done = bf16[1,192,4096]{2,1,0:T(8,128)(2,1)S(1)} copy-done((bf16[1,192,4096]{2,1,0:T(8,128)(2,1)S(1)}, bf16[1,192,4096]{2,1,0:T(8,128)(2,1)}, u32[]{:S(2)}) %copy-start) | copy-done | bytes 1572888
  2.9 0.0 copy-start.1
  3.0 1.4 %copy-done.1 = bf16[1,192,4096]{2,1,0:T(8,128)(2,1)S(1)} copy-done((bf16[1,192,4096]{2,1,0:T(8,128)(2,1)S(1)}, bf16[1,192,4096]{2,1,0:T(8,128)(2,1)}, u32[]{:S(2)}) %copy-start.1) | copy-done | bytes 1572888
  4.4 0.0 copy-start.2
  4.4 1.4 %copy-done.2 = bf16[1,1536,512]{2,1,0:T(8,128)(2,1)S(1)} copy-done((bf16[1,1536,512]{2,1,0:T(8,128)(2,1)S(1)}, bf16[1,1536,512]{2,1,0:T(8,128)(2,1)}, u32[]{:S(2)}) %copy-start.2) | copy-done | bytes 1572888
  5.8 0.0 copy-start.3
  5.8 0.8 copy-done.3
  6.6 122.2 %shard_map.64 = bf16[64,512]{1,0:T(8,128)(2,1)S(1)} custom-call(bf16[64,512]{1,0:T(8,128)(2,1)S(1)} %copy-done.3, bf16[192,4096]{1,0:T(8,128)(2,1)S(1)} %bitcast.3, bf16[192,4096]{1,0:T(8,128)(2,1)S(1)} %bitcast.4, bf16[1536,512]{1,0:T(8,128)(2,1)S(1)} %bitcast.5, s32[64,8]{1,0:T(8,128)S(1)} %copy.7.ids, f32[64,8]{1,0:T(8,128)S(1)} %copy.8.prob), custom_call_target="tpu_custom_call" | custom-call | flops 5000000000 | bytes 5000000 | tf_op jit(solution)/shard_map/pallas_call | solution.py:405
  128.8 0.6 copy.10
Async XLA Ops:
  1.5 1.4 %copy-start = (bf16[1,192,4096]{2,1,0:T(8,128)(2,1)S(1)}, bf16[1,192,4096]{2,1,0:T(8,128)(2,1)}, u32[]{:S(2)}) copy-start(bf16[1,192,4096]{2,1,0:T(8,128)(2,1)} %param.7) | copy-start | bytes 4718596
  2.9 1.4 %copy-start.1 = (bf16[1,192,4096]{2,1,0:T(8,128)(2,1)S(1)}, bf16[1,192,4096]{2,1,0:T(8,128)(2,1)}, u32[]{:S(2)}) copy-start(bf16[1,192,4096]{2,1,0:T(8,128)(2,1)} %param.8) | copy-start | bytes 4718596
  4.4 1.4 %copy-start.2 = (bf16[1,1536,512]{2,1,0:T(8,128)(2,1)S(1)}, bf16[1,1536,512]{2,1,0:T(8,128)(2,1)}, u32[]{:S(2)}) copy-start(bf16[1,1536,512]{2,1,0:T(8,128)(2,1)} %param.9) | copy-start | bytes 4718596
  5.8 0.8 copy-start.3

commit v2 on v0

v2 whole, which is shorter than its diff:
```python
import functools

import jax
import jax.numpy as jnp
from jax import lax
from jax.experimental import pallas as pl
from jax.experimental.pallas import tpu as pltpu
from jax.sharding import PartitionSpec as P

MESH = pl.DeviceIdType.MESH
BF16 = jnp.bfloat16
F32 = jnp.float32
NX, NY, NZ, NC = 4, 8, 8, 2
ROW = NX * NC
ROWS = 64
SLOTS = 16
SLICE = 512
HALF = 2048
HID = 192
PIECE = HID // 2
META = 128
FIRST = META + SLICE
REST = HALF - SLICE
PLACES = (0, 6, 2, 4)
GROUP_ROWS = ROW * SLOTS

ORDER = (
    "M0", "M1", "M2", "G1", "G2", "V0", "M3", "M4", "G3", "M5", "M6", "Z1",
    "Z2", "M7", "B2", "Z3", "Z4", "B3", "B4", "W0", "A0", "A2", "Z5", "Z6",
    "B5", "S0", "B6", "A3", "S2", "Z7", "B7", "10", "B1", "A4", "S3", "12",
    "20", "A5", "S4", "13", "22", "30", "A6", "S5", "14", "23", "32", "A7",
    "S6", "P0", "15", "24", "33", "A1", "S7", "P2", "16", "C0", "25", "34",
    "P3", "S1", "17", "C2", "26", "35", "P4", "11", "C3", "27", "36", "P5",
    "21", "C4", "37", "P6", "31", "C5", "P7", "C6", "P1", "C7", "D0", "D2",
    "D3", "D4", "D5", "D6", "D7", "C1",
)
DIRECT = ()


def dot(a, b, da, db):
    return lax.dot_general(a, b, (((da,), (db,)), ((), ())), preferred_element_type=F32)


def kernel(
    tok, gate, up, down, ids, prob, out,
    blocks, picked, arrived, weights, down_v, own, part_out, part_in,
    hidden, outputs, returned, sums_out, sums_in, own_sum, ids_v, prob_v,
    lt, pg_s, pg_r, w_s, w_r, lw, ld, zs_s, zs_r, zf_s, zf_r, z_s, z_r, xs_s, xs_r, xf_s, xf_r, x_s, x_r, p_s, p_r, h_s, h_r, o_s, o_r, f_s, f_r,
):
    t = lax.axis_index("tensor")
    e = lax.axis_index("expert")
    c = lax.rem(e, NC)
    z = lax.rem(e // NC, NZ)
    x = e // (NC * NZ)
    me = x * NC + c

    def along_y(step):
        return (lax.rem(t + step + NY, NY), e)

    def along_z(step):
        return (t, (x * NZ + lax.rem(z + step + NZ, NZ)) * NC + c)

    def in_row(j):
        return (t, ((j // NC) * NZ + z) * NC + lax.rem(j, NC))

    def other(i):
        return lax.rem(me + i, ROW)

    def send(src, dst, ss, rs, dev):
        return pltpu.make_async_remote_copy(
            src_ref=src, dst_ref=dst, send_sem=ss, recv_sem=rs, device_id=dev, device_id_type=MESH
        )

    def got(ref, sem):
        send(ref, ref, sem, sem, along_y(1)).wait_recv()

    def sent(ref, sem):
        send(ref, ref, sem, sem, along_y(1)).wait_send()

    def offset(d):
        return ((d + 1) // 2) * (1 - 2 * lax.rem(d + 1, 2))

    barrier = pltpu.get_barrier_semaphore()
    for step in range(1, NY):
        pl.semaphore_signal(barrier, inc=1, device_id=along_y(step), device_id_type=MESH)
    for i in range(1, ROW):
        pl.semaphore_signal(barrier, inc=1, device_id=in_row(other(i)), device_id_type=MESH)
    for step in range(1, NZ):
        pl.semaphore_signal(barrier, inc=1, device_id=along_z(step), device_id_type=MESH)
    def column(tensor, p):
        return pl.ds(pl.multiple_of(lax.rem(tensor + PLACES[p], NY) * SLICE, SLICE), SLICE)

    def place(p):
        return pl.ds(META + p * SLICE, SLICE)

    local = []
    for a, ref in enumerate((gate, up)):
        for p in range(4):
            local.append(
                pltpu.make_async_copy(
                    ref.at[:, column(t, p)],
                    weights.at[pl.ds(a * HID, HID), pl.ds(p * SLICE, SLICE)],
                    lw.at[a, p],
                )
            )
    local.append(pltpu.make_async_copy(down, down_v, ld.at[0]))
    first = [
        pltpu.make_async_copy(ids, ids_v, lt.at[0]),
        pltpu.make_async_copy(prob, prob_v, lt.at[1]),
        pltpu.make_async_copy(tok, blocks.at[0, :, place(0)], lt.at[2]),
    ]
    for cp in first + local:
        cp.start()
    for cp in first:
        cp.wait()

    lane = lax.broadcasted_iota(jnp.int32, (ROWS, META), 1).astype(F32)
    p_t = prob_v[...]
    p_hi = p_t.astype(BF16).astype(F32)
    terms = jnp.concatenate([ids_v[...].astype(F32), jnp.zeros((8, ROWS), F32), p_hi, p_t - p_hi], axis=0)
    put = (
        lax.broadcasted_iota(jnp.int32, (32, META), 0) == lax.broadcasted_iota(jnp.int32, (32, META), 1)
    ).astype(F32)
    meta = dot(terms.astype(BF16), put.astype(BF16), 0, 0)
    idf = meta[:, 0:8]
    named = jnp.zeros((ROWS, META), F32)
    for k in range(8):
        named = named + (lane == idf[:, k : k + 1]).astype(F32)
    earlier = (
        lax.broadcasted_iota(jnp.int32, (ROWS, ROWS), 1)
        < lax.broadcasted_iota(jnp.int32, (ROWS, ROWS), 0)
    ).astype(F32)
    before = dot(earlier.astype(BF16), named.astype(BF16), 1, 0)
    for k in range(8):
        ek = idf[:, k : k + 1]
        slot = jnp.sum(jnp.where(lane == ek, before, 0.0), axis=1, keepdims=True)
        meta = jnp.where(lane == float(8 + k), slot, meta)
    blocks[0, :, pl.ds(0, META)] = meta.astype(BF16)
    lane_i = lax.broadcasted_iota(jnp.int32, (ROWS, META), 1)
    lane_j = lane_i // SLOTS
    lane_e = ((lane_j // NC) * NZ + z) * NC + lax.rem(lane_j, NC)
    lane_code = (lane_e * SLOTS + lax.rem(lane_i, SLOTS)).astype(F32)

    def matches(m):
        return [
            (m[:, k : k + 1] * float(SLOTS) + m[:, 8 + k : 9 + k]) == lane_code for k in range(8)
        ]

    def picks(m):
        pick = functools.reduce(jnp.logical_or, matches(m))
        return jnp.where(pick, 1.0, 0.0).astype(BF16)

    own_pick = picks(meta)

    def pick(d, mask, p, n):
        rows = dot(mask, blocks[d, :, pl.ds(META + p * SLICE, n * SLICE)], 0, 0).astype(BF16)
        cols = pl.ds(p * SLICE, n * SLICE)
        picked[d, :, :, cols] = rows.reshape(ROW, SLOTS, n * SLICE)
        arrived[d, me, :, cols] = picked[d, me, :, cols]

    def send_row(d, p, n, ss, rs):
        cols = pl.ds(p * SLICE, n * SLICE)
        for i in range(1, ROW):
            j = other(i)
            send(
                picked.at[d, j, :, cols], arrived.at[d, me, :, cols], ss.at[j], rs.at[me], in_row(j)
            ).start()

    def pass_on(d, cols, ss, rs):
        way = 1 - 2 * (d % 2)
        if d in (5, 6):
            part = pl.ds(32 * (d - 5), 32)
            send(
                blocks.at[d, part, cols], blocks.at[7, part, cols],
                ss.at[d + 2], rs.at[d + 2], along_z(way),
            ).start()
        elif d < 5:
            send(
                blocks.at[d, :, cols], blocks.at[d + 2, :, cols],
                ss.at[d + 2], rs.at[d + 2], along_z(way),
            ).start()

    def block_there(d, cols, rs):
        if d == 7:
            for part in range(2):
                got(blocks.at[7, pl.ds(32 * part, 32), cols], rs.at[7 + part])
        else:
            got(blocks.at[d, :, cols], rs.at[d])

    first_cols = pl.ds(0, FIRST)
    rest_cols = pl.ds(FIRST, REST)

    def mask_of(d):
        return own_pick if d == 0 else picks(blocks[d, :, pl.ds(0, META)].astype(F32))

    def first_step(d):
        if d == 0:
            for way in range(2):
                send(
                    blocks.at[0, :, first_cols], blocks.at[1 + way, :, first_cols],
                    zf_s.at[1 + way], zf_r.at[1 + way], along_z(2 * way - 1),
                ).start()
        else:
            block_there(d, first_cols, zf_r)
            pass_on(d, first_cols, zf_s, zf_r)
            pick(d, mask_of(d), 0, 1)
        send_row(d, 0, 1, xf_s.at[d], xf_r.at[d])

    def gather_step(p):
        got(blocks.at[0, :, place(p)], pg_r.at[p - 1])
        for way in range(2):
            send(
                blocks.at[0, :, place(p)], blocks.at[1 + way, :, place(p)],
                zs_s.at[way, p - 1], zs_r.at[way, p - 1], along_z(2 * way - 1),
            ).start()
        pick(0, own_pick, p, 1)
        send_row(0, p, 1, xs_s.at[p - 1], xs_r.at[p - 1])

    def rest_step(d):
        if d <= 2:
            for p in range(1, 4):
                got(blocks.at[d, :, place(p)], zs_r.at[d - 1, p - 1])
        else:
            block_there(d, rest_cols, z_r)
        pass_on(d, rest_cols, z_s, z_r)

    def block_step(d):
        pick(d, mask_of(d), 1, 3)
        send_row(d, 1, 3, x_s.at[d], x_r.at[d])

    pick(0, own_pick, 0, 1)
    pl.semaphore_wait(barrier, NY + ROW + NZ - 3)

    for p in (3, 1, 2):
        send(
            blocks.at[0, :, place(0)], blocks.at[0, :, place(p)],
            pg_s.at[p - 1], pg_r.at[p - 1], along_y(-PLACES[p]),
        ).start()

    def swap_weights():
        for a, ref in enumerate((gate, up)):
            for p in range(4):
                to = pl.ds(p * SLICE, SLICE)
                send(
                    ref.at[pl.ds(0, PIECE), column(t + NY - 1, p)],
                    weights.at[pl.ds(3 * HID + a * PIECE, PIECE), to],
                    w_s.at[0, a, p], w_r.at[0, a, p], along_y(-1),
                ).start()
                send(
                    ref.at[pl.ds(PIECE, PIECE), column(t + 1, p)],
                    weights.at[pl.ds(2 * HID + a * PIECE, PIECE), to],
                    w_s.at[1, a, p], w_r.at[1, a, p], along_y(1),
                ).start()

    def weights_there():
        for cp in local:
            cp.wait()
        for a in range(2):
            for j in range(4):
                to = pl.ds(j * SLICE, SLICE)
                got(weights.at[pl.ds(3 * HID + a * PIECE, PIECE), to], w_r.at[0, a, j])
                got(weights.at[pl.ds(2 * HID + a * PIECE, PIECE), to], w_r.at[1, a, j])

    def partials(g):
        for i in range(1, ROW):
            src = other(i)
            got(arrived.at[g, src, :, pl.ds(0, SLICE)], xf_r.at[g, src])
            if g == 0:
                for p in range(1, 4):
                    got(arrived.at[0, src, :, pl.ds(p * SLICE, SLICE)], xs_r.at[p - 1, src])
            else:
                got(arrived.at[g, src, :, pl.ds(SLICE, REST)], x_r.at[g, src])
        rows = arrived[g].reshape(GROUP_ROWS, HALF)
        part = dot(weights[pl.ds(2 * HID, 2 * HID)], rows, 1, 1).astype(BF16)
        for side in range(2):
            part_out[g, side] = part[side * HID : (side + 1) * HID]
            send(
                part_out.at[g, side], part_in.at[g, 1 - side],
                p_s.at[g, side], p_r.at[g, 1 - side], along_y(2 * side - 1),
            ).start()
        own[g] = dot(weights[pl.ds(0, 2 * HID)], rows, 1, 1)

    def activate(g):
        for side in range(2):
            got(part_in.at[g, side], p_r.at[g, side])
            lo = pl.ds(side * PIECE, PIECE)
            gv = own[g, lo] + part_in[g, side, pl.ds(0, PIECE)].astype(F32)
            uv = own[g, pl.ds(HID + side * PIECE, PIECE)] + part_in[
                g, side, pl.ds(PIECE, PIECE)
            ].astype(F32)
            hidden[g, t, lo] = (gv / (1.0 + jnp.exp(-gv)) * uv).astype(BF16)
        if g in DIRECT:
            for step in (4, 1, 7, 2, 6, 3, 5):
                sem = (step // 5, 3 - abs(4 - step) if step < 5 else 7 - step)
                send(
                    hidden.at[g, t], hidden.at[g, t], h_s.at[g, sem[0], sem[1]],
                    h_r.at[g, sem[0], sem[1]], along_y(step),
                ).start()
            return
        for way in range(2):
            send(
                hidden.at[g, t], hidden.at[g, t], h_s.at[g, way, 0], h_r.at[g, way, 0],
                along_y(1 - 2 * way),
            ).start()

    def forward(g, h):
        for way in range(2):
            src = lax.rem(t + (h if way else NY - h), NY)
            ref = hidden.at[g, src]
            got(ref, h_r.at[g, way, h - 1])
            if h == 3:
                ref = hidden.at[g, src, pl.ds(way * PIECE, PIECE)]
            send(ref, ref, h_s.at[g, way, h], h_r.at[g, way, h], along_y(1 - 2 * way)).start()

    def project(g):
        if g in DIRECT:
            for step in range(1, NY):
                sem = (step // 5, 3 - abs(4 - step) if step < 5 else 7 - step)
                got(hidden.at[g, lax.rem(t + NY - step, NY)], h_r.at[g, sem[0], sem[1]])
        else:
            far = lax.rem(t + 4, NY)
            for way in range(2):
                got(hidden.at[g, far, pl.ds(way * PIECE, PIECE)], h_r.at[g, way, 3])
        h = hidden[g].reshape(NY * HID, GROUP_ROWS)
        o = dot(h, down_v[...], 0, 0).astype(BF16)
        outputs[g] = o.reshape(ROW, SLOTS, SLICE)
        returned[g, me] = outputs[g, me]
        for i in range(1, ROW):
            j = other(i)
            send(
                outputs.at[g, j], returned.at[g, me], o_s.at[g, j], o_r.at[g, me], in_row(j)
            ).start()

    def combine(g):
        for i in range(1, ROW):
            src = other(i)
            got(returned.at[g, src], o_r.at[g, src])
        m = blocks[g, :, pl.ds(0, META)].astype(F32)
        hi = jnp.zeros((ROWS, META), F32)
        lo = jnp.zeros((ROWS, META), F32)
        for k, match in enumerate(matches(m)):
            hi = jnp.where(match, m[:, 16 + k : 17 + k], hi)
            lo = jnp.where(match, m[:, 24 + k : 25 + k], lo)
        vals = returned[g].reshape(GROUP_ROWS, SLICE)
        total = dot(hi.astype(BF16), vals, 1, 0) + dot(lo.astype(BF16), vals, 1, 0)
        sums_out[g] = total.astype(BF16)

        if g == 0:
            own_sum[...] = total
        else:
            send(sums_out.at[g], sums_in.at[g], f_s.at[g], f_r.at[g], along_z(offset(g))).start()

    def drain(g):
        for i in range(1, ROW):
            j = other(i)
            sent(picked.at[g, j, :, pl.ds(0, SLICE)], xf_s.at[g, j])
            if g == 0:
                for p in range(1, 4):
                    sent(picked.at[0, j, :, pl.ds(p * SLICE, SLICE)], xs_s.at[p - 1, j])
            else:
                sent(picked.at[g, j, :, pl.ds(SLICE, REST)], x_s.at[g, j])
        for side in range(2):
            sent(part_out.at[g, side], p_s.at[g, side])
            for h in range(3):
                sent(hidden.at[g, 0], h_s.at[g, side, h])
        if g in DIRECT:
            sent(hidden.at[g, 0], h_s.at[g, 0, 3])
        else:
            for side in range(2):
                sent(hidden.at[g, 0, pl.ds(0, PIECE)], h_s.at[g, side, 3])
        for i in range(1, ROW):
            j = other(i)
            sent(outputs.at[g, j], o_s.at[g, j])

    run = {
        "M": first_step, "G": gather_step, "Z": rest_step, "B": block_step, "V": lambda k: swap_weights(), "A": partials, "S": activate, "P": project, "C": combine, "D": drain,
        "1": lambda k: forward(k, 1), "2": lambda k: forward(k, 2), "3": lambda k: forward(k, 3),
        "W": lambda k: weights_there(),
    }
    for step in ORDER:
        run[step[0]](int(step[1]))

    drain(1)
    for i in range(3):
        sent(blocks.at[0, :, place(0)], pg_s.at[i])
    for a in range(2):
        for j in range(4):
            for way in range(2):
                sent(weights.at[pl.ds(0, PIECE), pl.ds(0, SLICE)], w_s.at[way, a, j])
    for way in range(2):
        for p in range(1, 4):
            sent(blocks.at[0, :, place(p)], zs_s.at[way, p - 1])
        sent(blocks.at[0, :, first_cols], zf_s.at[1 + way])
    for d in range(3, 7):
        sent(blocks.at[d, :, first_cols], zf_s.at[d])
        sent(blocks.at[d, :, rest_cols], z_s.at[d])
    for d in (7, 8):
        sent(blocks.at[7, pl.ds(0, 32), first_cols], zf_s.at[d])
        sent(blocks.at[7, pl.ds(0, 32), rest_cols], z_s.at[d])

    total = own_sum[...]
    for d in (2, 3, 4, 5, 6, 7, 1):
        got(sums_in.at[d], f_r.at[d])
        total = total + sums_in[d].astype(F32)
    out[...] = total.astype(BF16)
    for d in range(1, NZ):
        sent(sums_out.at[d], f_s.at[d])


def local(tokens, gate_weight, up_weight, down_weight, expert_ids, gate_probs):
    hbm = pl.BlockSpec(memory_space=pltpu.HBM)
    vmem = pl.BlockSpec(memory_space=pltpu.VMEM)
    dma = pltpu.SemaphoreType.DMA
    scratch = [
        pltpu.VMEM((NZ, ROWS, HALF + META), BF16),
        pltpu.VMEM((NZ, ROW, SLOTS, HALF), BF16),
        pltpu.VMEM((NZ, ROW, SLOTS, HALF), BF16),
        pltpu.VMEM((4 * HID, HALF), BF16),
        pltpu.VMEM((NY * HID, SLICE), BF16),
        pltpu.VMEM((NZ, 2 * HID, GROUP_ROWS), F32),
        pltpu.VMEM((NZ, 2, HID, GROUP_ROWS), BF16),
        pltpu.VMEM((NZ, 2, HID, GROUP_ROWS), BF16),
        pltpu.VMEM((NZ, NY, HID, GROUP_ROWS), BF16),
        pltpu.VMEM((NZ, ROW, SLOTS, SLICE), BF16),
        pltpu.VMEM((NZ, ROW, SLOTS, SLICE), BF16),
        pltpu.VMEM((NZ, ROWS, SLICE), BF16),
        pltpu.VMEM((NZ, ROWS, SLICE), BF16),
        pltpu.VMEM((ROWS, SLICE), F32),
        pltpu.VMEM((8, ROWS), jnp.int32),
        pltpu.VMEM((8, ROWS), F32),
        dma((3,)),
        dma((3,)), dma((3,)),
        dma((2, 2, 4)), dma((2, 2, 4)), dma((2, 4)), dma((1,)),
        dma((2, 3)), dma((2, 3)), dma((9,)), dma((9,)), dma((9,)), dma((9,)),
        dma((3, ROW)), dma((3, ROW)), dma((NZ, ROW)), dma((NZ, ROW)), dma((NZ, ROW)), dma((NZ, ROW)),
        dma((NZ, 2)), dma((NZ, 2)),
        dma((NZ, 2, 4)), dma((NZ, 2, 4)),
        dma((NZ, ROW)), dma((NZ, ROW)),
        dma((NZ,)), dma((NZ,)),
    ]
    return pl.pallas_call(
        kernel,
        out_shape=jax.ShapeDtypeStruct((ROWS, SLICE), BF16),
        in_specs=[hbm] * 6,
        out_specs=vmem,
        scratch_shapes=scratch,
        compiler_params=pltpu.CompilerParams(
            collective_id=0, has_side_effects=True, vmem_limit_bytes=(64 << 20) - (1 << 18)
        ),
        cost_estimate=pl.CostEstimate(flops=5_000_000_000, bytes_accessed=5_000_000, transcendentals=200_000),
    )(tokens, gate_weight[0], up_weight[0], down_weight[0], expert_ids.T, gate_probs.T)


def solution(mesh):
    in_specs = (
        P("expert", "tensor"),
        P("expert", "tensor", None),
        P("expert", "tensor", None),
        P("expert", None, "tensor"),
        P("expert", None),
        P("expert", None),
    )
    out_specs = P("expert", "tensor")
    return jax.shard_map(local, mesh=mesh, in_specs=in_specs, out_specs=out_specs, check_vma=False)
```

time: 343 us -> 109 us (0.32)
  blocking collectives: 228 us -> 0 us
  Pallas kernels: 0 us -> 107 us
  waiting for transfers between devices: 69.8 us -> 0 us
  matrix products: 15 us -> 0 us
  between operations: 13.5 us -> 0.01 us
  starting transfers between devices: 11.7 us -> 0 us
  other arithmetic: 3.49 us -> 0 us
    all_to_all x1 -> x0, blocking collectives: 206 us -> none  [local(): lax.all_to_all(sent, 'expert', split_axis=0, concat_axis=0, tiled=True)]
    pallas_call x0 -> x1, Pallas kernels: none -> 107 us  [local(): pl.pallas_call(kernel, out_shape=jax.ShapeDtypeStruct((ROWS, SLICE), BF16...]
    all_gather x1 -> x0, waiting for transfers between devices: 42.1 us -> none  [local(): lax.all_gather(hidden, 'tensor', axis=1, tiled=True)]
    all_to_all x1 -> x0, waiting for transfers between devices: 27.7 us -> none  [local(): lax.all_to_all(output.reshape(experts, slot_count, out_cols), 'expert', s...]
    all_gather x1 -> x0, blocking collectives: 21.9 us -> none  [local(): whole = lax.all_gather(tokens, 'tensor', axis=1, tiled=True)]
    dot_general x5 -> x0, matrix products: 15 us -> none  [the longest x1 4.7 us: local(): jnp.dot(lax.all_gather(hidden, 'tensor', axis=1, tiled=True), part_down,...]
    all_to_all x1 -> x0, starting transfers between devices: 11.7 us -> none  [local(): lax.all_to_all(output.reshape(experts, slot_count, out_cols), 'expert', s...]
  transfers between devices with their start and end apart: 2 -> 0, of which waited for: 2 -> 0; matrix products, arithmetic and copies ran while one was open for 0% -> 0% of each run, Pallas kernels for 0% -> 0%
where the time goes in v2:
time: 109 us
  Pallas kernels  107 us (98%)
  local copies, waits for them, and re-layouts  1.47 us (1%)
    pallas_call x1, Pallas kernels, local(): pl.pallas_call(kernel, out_shape=jax.ShapeDtypeStruct((ROWS, SLICE), BF16...  107 us

profile of v2, /device:TPU:1, one launch (start us, length us, event | category | flops | bytes accessed | tf_op | source)
XLA Modules:
  0.0 108.9 jit_solution(8089195958033312656)
XLA Ops:
  0.0 107.4 %shard_map.64 = bf16[64,512]{1,0:T(8,128)(2,1)} custom-call(bf16[64,512]{1,0:T(8,128)(2,1)} %tok.1, bf16[192,4096]{1,0:T(8,128)(2,1)} %bitcast.5, bf16[192,4096]{1,0:T(8,128)(2,1)} %bitcast.6, bf16[1536,512]{1,0:T(8,128)(2,1)} %bitcast.7, s32[8,64]{1,0:T(8,128)} %bitcast.8, f32[8,64]{1,0:T(8,128)} %bitcast.9), custom_call_target="tpu_custom_call" | custom-call | flops 5000000000 | bytes 5000000 | tf_op jit(solution)/shard_map/pallas_call | solution.py:441
  107.4 1.5 %copy.8 = bf16[64,512]{1,0:T(8,128)(2,1)} copy(bf16[64,512]{1,0:T(8,128)(2,1)} %shard_map.64) | data formatting | bytes 131072

commit v3 on v2

--- a/solution.py
+++ b/solution.py
@@ -25,7 +25,7 @@
 GROUP_ROWS = ROW * SLOTS
 
 ORDER = (
-    "M0", "M1", "M2", "G1", "G2", "V0", "M3", "M4", "G3", "M5", "M6", "Z1",
+    "M0", "V0", "M1", "M2", "G1", "G2", "M3", "M4", "G3", "M5", "M6", "Z1",
     "Z2", "M7", "B2", "Z3", "Z4", "B3", "B4", "W0", "A0", "A2", "Z5", "Z6",
     "B5", "S0", "B6", "A3", "S2", "Z7", "B7", "10", "B1", "A4", "S3", "12",
     "20", "A5", "S4", "13", "22", "30", "A6", "S5", "14", "23", "32", "A7",
@@ -34,7 +34,6 @@
     "21", "C4", "37", "P6", "31", "C5", "P7", "C6", "P1", "C7", "D0", "D2",
     "D3", "D4", "D5", "D6", "D7", "C1",
 )
-DIRECT = ()
 
 
 def dot(a, b, da, db):
@@ -81,11 +80,11 @@
         return ((d + 1) // 2) * (1 - 2 * lax.rem(d + 1, 2))
 
     barrier = pltpu.get_barrier_semaphore()
-    for step in range(1, NY):
+    for step in (4, 2, 6, 1, 7):
         pl.semaphore_signal(barrier, inc=1, device_id=along_y(step), device_id_type=MESH)
-    for i in range(1, ROW):
+    for i in (4, 5, 3, 2, 6, 7, 1):
         pl.semaphore_signal(barrier, inc=1, device_id=in_row(other(i)), device_id_type=MESH)
-    for step in range(1, NZ):
+    for step in (4, 3, 5, 2, 6, 1, 7):
         pl.semaphore_signal(barrier, inc=1, device_id=along_z(step), device_id_type=MESH)
     def column(tensor, p):
         return pl.ds(pl.multiple_of(lax.rem(tensor + PLACES[p], NY) * SLICE, SLICE), SLICE)
@@ -229,7 +228,7 @@
         send_row(d, 1, 3, x_s.at[d], x_r.at[d])
 
     pick(0, own_pick, 0, 1)
-    pl.semaphore_wait(barrier, NY + ROW + NZ - 3)
+    pl.semaphore_wait(barrier, 5 + 7 + 7)
 
     for p in (3, 1, 2):
         send(
@@ -289,14 +288,6 @@
                 g, side, pl.ds(PIECE, PIECE)
             ].astype(F32)
             hidden[g, t, lo] = (gv / (1.0 + jnp.exp(-gv)) * uv).astype(BF16)
-        if g in DIRECT:
-            for step in (4, 1, 7, 2, 6, 3, 5):
-                sem = (step // 5, 3 - abs(4 - step) if step < 5 else 7 - step)
-                send(
-                    hidden.at[g, t], hidden.at[g, t], h_s.at[g, sem[0], sem[1]],
-                    h_r.at[g, sem[0], sem[1]], along_y(step),
-                ).start()
-            return
         for way in range(2):
             send(
                 hidden.at[g, t], hidden.at[g, t], h_s.at[g, way, 0], h_r.at[g, way, 0],
@@ -313,14 +304,9 @@
             send(ref, ref, h_s.at[g, way, h], h_r.at[g, way, h], along_y(1 - 2 * way)).start()
 
     def project(g):
-        if g in DIRECT:
-            for step in range(1, NY):
-                sem = (step // 5, 3 - abs(4 - step) if step < 5 else 7 - step)
-                got(hidden.at[g, lax.rem(t + NY - step, NY)], h_r.at[g, sem[0], sem[1]])
-        else:
-            far = lax.rem(t + 4, NY)
-            for way in range(2):
-                got(hidden.at[g, far, pl.ds(way * PIECE, PIECE)], h_r.at[g, way, 3])
+        far = lax.rem(t + 4, NY)
+        for way in range(2):
+            got(hidden.at[g, far, pl.ds(way * PIECE, PIECE)], h_r.at[g, way, 3])
         h = hidden[g].reshape(NY * HID, GROUP_ROWS)
         o = dot(h, down_v[...], 0, 0).astype(BF16)
         outputs[g] = o.reshape(ROW, SLOTS, SLICE)
@@ -363,11 +349,8 @@
             sent(part_out.at[g, side], p_s.at[g, side])
             for h in range(3):
                 sent(hidden.at[g, 0], h_s.at[g, side, h])
-        if g in DIRECT:
-            sent(hidden.at[g, 0], h_s.at[g, 0, 3])
-        else:
-            for side in range(2):
-                sent(hidden.at[g, 0, pl.ds(0, PIECE)], h_s.at[g, side, 3])
+        for side in range(2):
+            sent(hidden.at[g, 0, pl.ds(0, PIECE)], h_s.at[g, side, 3])
         for i in range(1, ROW):
             j = other(i)
             sent(outputs.at[g, j], o_s.at[g, j])

time: 109 us -> 107 us (0.982)
    pallas_call x1, Pallas kernels: 107 us -> 106 us  [local(): pl.pallas_call(kernel, out_shape=jax.ShapeDtypeStruct((ROWS, SLICE), BF16...]
where the time goes in v3:
time: 107 us
  Pallas kernels  106 us (99%)
  local copies, waits for them, and re-layouts  1.47 us (1%)
    pallas_call x1, Pallas kernels, local(): pl.pallas_call(kernel, out_shape=jax.ShapeDtypeStruct((ROWS, SLICE), BF16...  106 us

profile of v3, /device:TPU:1, one launch (start us, length us, event | category | flops | bytes accessed | tf_op | source)
XLA Modules:
  0.0 107.0 jit_solution(7945466880715502518)
XLA Ops:
  0.0 105.6 %shard_map.64 = bf16[64,512]{1,0:T(8,128)(2,1)} custom-call(bf16[64,512]{1,0:T(8,128)(2,1)} %tok.1, bf16[192,4096]{1,0:T(8,128)(2,1)} %bitcast.5, bf16[192,4096]{1,0:T(8,128)(2,1)} %bitcast.6, bf16[1536,512]{1,0:T(8,128)(2,1)} %bitcast.7, s32[8,64]{1,0:T(8,128)} %bitcast.8, f32[8,64]{1,0:T(8,128)} %bitcast.9), custom_call_target="tpu_custom_call" | custom-call | flops 5000000000 | bytes 5000000 | tf_op jit(solution)/shard_map/pallas_call | solution.py:424
  105.6 1.5 %copy.8 = bf16[64,512]{1,0:T(8,128)(2,1)} copy(bf16[64,512]{1,0:T(8,128)(2,1)} %shard_map.64) | data formatting | bytes 131072

commit v4 on v3

--- a/solution.py
+++ b/solution.py
@@ -14,6 +14,7 @@
 ROW = NX * NC
 ROWS = 64
 SLOTS = 16
+FAR_FIRST = (4, 5, 3, 2, 6, 7, 1)
 SLICE = 512
 HALF = 2048
 HID = 192
@@ -82,7 +83,7 @@
     barrier = pltpu.get_barrier_semaphore()
     for step in (4, 2, 6, 1, 7):
         pl.semaphore_signal(barrier, inc=1, device_id=along_y(step), device_id_type=MESH)
-    for i in (4, 5, 3, 2, 6, 7, 1):
+    for i in FAR_FIRST:
         pl.semaphore_signal(barrier, inc=1, device_id=in_row(other(i)), device_id_type=MESH)
     for step in (4, 3, 5, 2, 6, 1, 7):
         pl.semaphore_signal(barrier, inc=1, device_id=along_z(step), device_id_type=MESH)
@@ -159,7 +160,7 @@
 
     def send_row(d, p, n, ss, rs):
         cols = pl.ds(p * SLICE, n * SLICE)
-        for i in range(1, ROW):
+        for i in FAR_FIRST:
             j = other(i)
             send(
                 picked.at[d, j, :, cols], arrived.at[d, me, :, cols], ss.at[j], rs.at[me], in_row(j)
@@ -311,7 +312,7 @@
         o = dot(h, down_v[...], 0, 0).astype(BF16)
         outputs[g] = o.reshape(ROW, SLOTS, SLICE)
         returned[g, me] = outputs[g, me]
-        for i in range(1, ROW):
+        for i in FAR_FIRST:
             j = other(i)
             send(
                 outputs.at[g, j], returned.at[g, me], o_s.at[g, j], o_r.at[g, me], in_row(j)

time: 107 us -> 107 us (level)
  no operation moved by 1% of the time
where the time goes in v4:
time: 107 us
  Pallas kernels  106 us (99%)
  local copies, waits for them, and re-layouts  1.47 us (1%)
    pallas_call x1, Pallas kernels, local(): pl.pallas_call(kernel, out_shape=jax.ShapeDtypeStruct((ROWS, SLICE), BF16...  106 us

profile of v4, /device:TPU:1, one launch (start us, length us, event | category | flops | bytes accessed | tf_op | source)
XLA Modules:
  0.0 107.2 jit_solution(17622714301131682720)
XLA Ops:
  0.0 105.8 %shard_map.64 = bf16[64,512]{1,0:T(8,128)(2,1)} custom-call(bf16[64,512]{1,0:T(8,128)(2,1)} %tok.1, bf16[192,4096]{1,0:T(8,128)(2,1)} %bitcast.5, bf16[192,4096]{1,0:T(8,128)(2,1)} %bitcast.6, bf16[1536,512]{1,0:T(8,128)(2,1)} %bitcast.7, s32[8,64]{1,0:T(8,128)} %bitcast.8, f32[8,64]{1,0:T(8,128)} %bitcast.9), custom_call_target="tpu_custom_call" | custom-call | flops 5000000000 | bytes 5000000 | tf_op jit(solution)/shard_map/pallas_call | solution.py:425
  105.8 1.5 %copy.8 = bf16[64,512]{1,0:T(8,128)(2,1)} copy(bf16[64,512]{1,0:T(8,128)(2,1)} %shard_map.64) | data formatting | bytes 131072
